TPU v7x, 32 devices: a whole 2x2x4 slice. The times are simulated.
32 devices in a mesh: tm: 8 (over z, y), sub: 4 (over x, core).
Axes of the slice: x: 2, y: 2, z: 4, core: 2. Of those that a mesh axis runs over, the one named last changes fastest.
Arguments:
- frames: bfloat16 [8192, 1024], P(('tm', 'sub')), may hold values from -16 to 16
- modulation: float32 [8, 1024], replicated, may hold values from -4 to 4
- w_project: bfloat16 [3, 1024, 1024], P(None, None, 'sub'), may hold values from -1 to 1
- w_heads_out: bfloat16 [1024, 1024], P('sub'), may hold values from -0.25 to 0.25
- w_up: bfloat16 [1024, 4096], P(None, 'sub'), may hold values from -0.1875 to 0.1875
- w_down: bfloat16 [4096, 1024], P('sub'), may hold values from -0.125 to 0.125
- w_velocity: bfloat16 [1024, 100], replicated, may hold values from -0.1875 to 0.1875
- noisy_mel: float32 [8192, 100], P('tm'), may hold values from -6 to 6
- w_prelude: bfloat16 [7, 1536, 100], P(None, 'sub'), may hold values from -0.21875 to 0.21875
- w_upsample: bfloat16 [8, 1536, 768], P(None, 'sub'), may hold values from -0.109375 to 0.109375
- snake_alpha: float32 [2, 768], replicated, may hold values from 0.3 to 3
- w_dilated: bfloat16 [3, 768, 768], P(None, 'sub'), may hold values from -0.125 to 0.125
- w_plain: bfloat16 [3, 768, 768], P(None, 'sub'), may hold values from -0.125 to 0.125
Outputs:
- mel_next: float32 [8192, 100], P('tm')
- section_out: bfloat16 [32768, 768], P(('tm', 'sub'))
All inputs are finite; a program needn't handle non-finite values.
Results may differ from a plain program's by a relative error of at most 0.03.
Values may be sent and summed in bfloat16 or wider, within the bound.
A program may use at most 64 MiB of HBM per device.

v0:
```python
import math

import jax
import jax.numpy as jnp
from jax import lax
from jax.sharding import PartitionSpec as P

HEAD_DIM = 64
BLK = 256


epsilon = 1e-06


def from_behind(block, axis, distance):
    devices = range(lax.axis_size(axis))
    route = [(i - distance, i) for i in devices if i - distance in devices]
    return lax.ppermute(block, axis, route)


def extended_2(cells, sides, width):
    for axis, dim in sides:
        count = lax.axis_size(axis)
        ends = count - 1
        head = lax.slice_in_dim(cells, 0, width, axis=dim)
        tail = lax.slice_in_dim(cells, cells.shape[dim] - width, cells.shape[dim], axis=dim)
        cells = jnp.concatenate(
            [
                lax.ppermute(tail, axis, [(i, (i + 1) % count) for i in range(ends)]),
                cells,
                lax.ppermute(head, axis, [((i + 1) % count, i) for i in range(ends)]),
            ],
            axis=dim,
        )
    return cells


def norm_rows(rows, offset_row, scale_row):
    rows = rows.astype(jnp.float32)
    center = jnp.mean(rows, axis=-1, keepdims=True)
    square = jnp.mean(rows * rows, axis=-1, keepdims=True)
    spread = square - center * center
    return (rows - center) * lax.rsqrt(spread + epsilon) * (1.0 + scale_row) + offset_row


def snake_act(values, alpha_row):
    return values + jnp.square(jnp.sin(alpha_row * values)) / alpha_row


def contract_first(left, right):
    return lax.dot_general(
        left, right, (((0,), (0,)), ((), ())), preferred_element_type=jnp.float32
    )


def phase_terms(prelude_cols, tap_weights, first_frame, span):
    current = lax.dynamic_slice_in_dim(prelude_cols, 1, span, 1)
    earlier = lax.dynamic_slice_in_dim(prelude_cols, first_frame, span, 1)
    later_frames = lax.dynamic_slice_in_dim(prelude_cols, 2, span, 1)

    def tap_product(source, offset):
        return contract_first(source, tap_weights[offset])

    phases = jnp.stack(
        [
            tap_product(current, 2) + tap_product(earlier, 6),
            tap_product(current, 3) + tap_product(earlier, 7),
            tap_product(current, 4) + tap_product(later_frames, 0),
            tap_product(current, 5) + tap_product(later_frames, 1),
        ],
        1,
    )
    return phases.reshape((4 * span, phases.shape[2]))


def block_attention(queries, keys_now, values_now, lookback, is_first):
    frame_count = queries.shape[0]
    head_count = queries.shape[1] // HEAD_DIM
    blocks = frame_count // BLK
    block_shape = (blocks, BLK, head_count, HEAD_DIM)
    edge_shape = (1, BLK, head_count, HEAD_DIM)
    key_blocks = keys_now.reshape(block_shape)
    value_blocks = values_now.reshape(block_shape)
    key_all = jnp.concatenate(
        [jnp.concatenate([lookback[0].reshape(edge_shape), key_blocks[:-1]], 0), key_blocks], 1
    )
    value_all = jnp.concatenate(
        [jnp.concatenate([lookback[1].reshape(edge_shape), value_blocks[:-1]], 0), value_blocks], 1
    )
    scores = jnp.einsum(
        "bqhd,bkhd->bhqk", queries.reshape(block_shape), key_all, preferred_element_type=jnp.float32
    ) / math.sqrt(HEAD_DIM)
    block_ids = lax.broadcasted_iota(jnp.int32, (blocks, 1, 1, 2 * BLK), 0)
    key_ids = lax.broadcasted_iota(jnp.int32, (blocks, 1, 1, 2 * BLK), 3)
    allowed = (block_ids > 0) | (key_ids >= BLK) | jnp.logical_not(is_first)
    scores = jnp.where(allowed, scores, -1e30)
    largest = jnp.max(scores, axis=-1, keepdims=True)
    raised = jnp.exp(scores - largest)
    weights = (raised / jnp.sum(raised, axis=-1, keepdims=True)).astype(jnp.bfloat16)
    attended = jnp.einsum("bhqk,bkhd->bqhd", weights, value_all, preferred_element_type=jnp.float32)
    return attended.reshape((frame_count, head_count * HEAD_DIM)).astype(jnp.bfloat16)


def dilated_conv(extended, row_count, w_dilated):
    empty_sum = jnp.zeros((row_count, w_dilated.shape[2]), jnp.float32)
    running = empty_sum
    weight_rows = lax.all_gather(w_dilated, "sub", axis=1, tiled=True)
    for offset in range(3):
        running = running + jnp.dot(
            extended[3 * offset : 3 * offset + row_count],
            weight_rows[offset],
            preferred_element_type=jnp.float32,
        )
    return running


def plain_conv(extended, row_count, w_plain):
    empty_sum = jnp.zeros((row_count, w_plain.shape[2]), jnp.float32)
    running = empty_sum
    weight_rows = lax.all_gather(w_plain, "sub", axis=1, tiled=True)
    for offset in range(3):
        running = running + jnp.dot(
            extended[offset : offset + row_count],
            weight_rows[offset],
            preferred_element_type=jnp.float32,
        )
    return running


def body(
    frames,
    modulation,
    w_project,
    w_heads_out,
    w_up,
    w_down,
    w_velocity,
    noisy_mel,
    w_prelude,
    w_upsample,
    snake_alpha,
    w_dilated,
    w_plain,
):
    own_rows = frames.shape[0]
    sub_index = lax.axis_index("sub")
    time_index = lax.axis_index("tm")
    gathered = lax.all_gather(frames, "sub", axis=0, tiled=True)
    frame_count = gathered.shape[0]
    first_norm = norm_rows(gathered, modulation[0], modulation[1]).astype(jnp.bfloat16)
    projected = jnp.einsum(
        "td,kde->kte", first_norm, w_project, preferred_element_type=jnp.float32
    ).astype(jnp.bfloat16)
    lookback = from_behind(
        (projected[1, frame_count - BLK :], projected[2, frame_count - BLK :]), "tm", 1
    )
    heads_out = block_attention(projected[0], projected[1], projected[2], lookback, time_index == 0)
    attn = lax.psum_scatter(
        jnp.dot(heads_out, w_heads_out, preferred_element_type=jnp.float32).astype(jnp.bfloat16),
        "sub",
        scatter_dimension=0,
        tiled=True,
    ).astype(jnp.float32)
    mixed_rows = (frames.astype(jnp.float32) + modulation[2] * attn).astype(jnp.bfloat16)
    own_norm = norm_rows(mixed_rows, modulation[3], modulation[4]).astype(jnp.bfloat16)
    second_norm = lax.all_gather(own_norm, "sub", axis=0, tiled=True)
    hidden = jax.nn.gelu(
        jnp.dot(second_norm, w_up, preferred_element_type=jnp.float32), approximate=True
    ).astype(jnp.bfloat16)
    feed = lax.psum_scatter(
        jnp.dot(hidden, w_down, preferred_element_type=jnp.float32).astype(jnp.bfloat16),
        "sub",
        scatter_dimension=0,
        tiled=True,
    ).astype(jnp.float32)
    final_rows = (mixed_rows.astype(jnp.float32) + modulation[5] * feed).astype(jnp.bfloat16)
    final_norm = norm_rows(final_rows, modulation[6], modulation[7]).astype(jnp.bfloat16)
    velocity = jnp.dot(final_norm, w_velocity, preferred_element_type=jnp.float32)
    noisy_own = lax.dynamic_slice_in_dim(noisy_mel, sub_index * own_rows, own_rows, 0)
    mel_own = noisy_own + 0.5 * velocity
    mel_next = lax.all_gather(mel_own, "sub", axis=0, tiled=True)
    mel_low = mel_next.astype(jnp.bfloat16)
    mel_wide = extended_2(mel_low, (("tm", 0),), 4)
    columns = frame_count + 2
    prelude = jnp.zeros((w_prelude.shape[1], columns), jnp.float32)
    for offset in range(7):
        prelude = prelude + lax.dot_general(
            w_prelude[offset],
            mel_wide[offset : offset + columns],
            (((1,), (1,)), ((), ())),
            preferred_element_type=jnp.float32,
        )
    frame_pos = time_index * frame_count - 1 + lax.broadcasted_iota(jnp.int32, (1, columns), 1)
    inside = (frame_pos >= 0) & (frame_pos < lax.axis_size("tm") * frame_count)
    prelude = jnp.where(inside, prelude, 0.0).astype(jnp.bfloat16)
    samples_dev = 4 * own_rows
    up_x = lax.psum_scatter(
        phase_terms(
            prelude, w_upsample, jnp.int32(0) // 4, samples_dev * lax.axis_size("sub") // 4
        ).astype(jnp.bfloat16),
        "sub",
        scatter_dimension=0,
        tiled=True,
    )
    wide_up = extended_2(up_x, ((("tm", "sub"), 0),), 4)
    act_one = snake_act(wide_up.astype(jnp.float32), snake_alpha[0]).astype(jnp.bfloat16)
    inner_conv = dilated_conv(act_one, samples_dev + 2, w_dilated)
    sample_pos = (
        (time_index * lax.axis_size("sub") + sub_index) * samples_dev
        - 1
        + lax.broadcasted_iota(jnp.int32, (samples_dev + 2, 1), 0)
    )
    within = (sample_pos >= 0) & (
        sample_pos < lax.axis_size("tm") * lax.axis_size("sub") * samples_dev
    )
    act_two = jnp.where(within, snake_act(inner_conv, snake_alpha[1]), 0.0).astype(jnp.bfloat16)
    outer_conv = plain_conv(act_two, samples_dev, w_plain)
    section_out = (up_x.astype(jnp.float32) + outer_conv).astype(jnp.bfloat16)
    return (mel_next, section_out)


def solution(mesh):
    in_specs = (
        P(("tm", "sub"), None),
        P(),
        P(None, None, "sub"),
        P("sub", None),
        P(None, "sub"),
        P("sub", None),
        P(),
        P("tm", None),
        P(None, "sub", None),
        P(None, "sub", None),
        P(),
        P(None, "sub", None),
        P(None, "sub", None),
    )
    out_specs = (P("tm", None), P(("tm", "sub"), None))
    return jax.shard_map(body, mesh=mesh, in_specs=in_specs, out_specs=out_specs, check_vma=False)
```

profile of v0, /device:TPU:0, one launch (start us, length us, event | category | flops | bytes accessed | tf_op | source)
XLA Modules:
  0.0 367.3 jit_solution(13628211951912956205)
XLA Ops:
  10.4 24.4 %all-gather.5.cloned.1.call-done = bf16[1024,1024]{1,0:T(8,128)(2,1)} async-done(((bf16[256,1024]{1,0:T(8,128)(2,1)}), bf16[1024,1024]{1,0:T(8,128)(2,1)}) %all-gather.5.cloned.1.call-update) | async-done | bytes 2097168 | tf_op jit(solution)/shard_map/all_gather | solution.py:148
  37.2 4.1 %fusion.61 = bf16[3,1024,256]{2,1,0:T(8,128)(2,1)S(1)} fusion(bf16[3,1024,256]{2,1,0:T(8,128)(2,1)} %param.15, bf16[1024,1024]{1,0:T(8,128)(2,1)} %all-gather.5.cloned.1.call-done, f32[1024]{0:T(1024)S(1)} %bitcast.122, f32[1024]{0:T(1024)S(1)} %bitcast.123, f32[1024]{0:T(1024)S(1)} %get-tuple-element.32, f32[1024]{0:T(1024)S(1)} %get-tuple-element.31), kind=kOutput, calls=%fused_computation.81 | convolution fusion | flops 1617690624 | bytes 5259264 | tf_op jit(solution)/shard_map/td,kde->kte/dot_general | solution.py:151
  49.7 4.0 %collective-permute-start.1 = (bf16[256,256]{1,0:T(8,128)(2,1)}, bf16[256,256]{1,0:T(8,128)(2,1)}, u32[]{:S(2)}, u32[]{:S(2)}) collective-permute-start(bf16[256,256]{1,0:T(8,128)(2,1)} %get-tuple-element.15), channel_id=1, source_target_pairs={{0,4},{4,8},{8,12},{12,16},{16,20},{20,24},{24,28},{1,5},{5,9},{9,... | collective-permute-start | bytes 393224 | tf_op jit(solution)/shard_map/ppermute | solution.py:18
  62.6 2.9 collective-permute-start
  66.5 7.4 %fusion.194 = (f32[4,4,256]{2,1,0:T(4,128)S(1)}, f32[4,4,256,512]{3,2,1,0:T(8,128)}) fusion(pred[4,512]{1,0:T(4,128)(4,1)} %or_or_fusion, bf16[4,256,4,64]{3,2,1,0:T(4,128)(2,1)} %reshape.121, bf16[4,256,4,64]{1,3,2,0:T(8,128)(2,1)} %copy.32, bf16[3,256,4,64]{1,3,2,0:T(8,128)(2,1)} %copy.30, bf16[1,256,4,64]{1,3,2,0:T(8,128)(2,1)S(1)} %bitcast.114), kind=kOutput, calls=%fused_computation.233 | convolution fusion | flops 279970304 | bytes 9979904 | tf_op jit(solution)/shard_map/sub | solution.py:98
  74.1 4.9 %fusion.69 = bf16[4,256,4,64]{1,3,2,0:T(8,128)(2,1)S(1)} fusion(f32[4,4,256,512]{3,2,1,0:T(8,128)} %get-tuple-element.38, f32[4,4,256]{2,1,0:T(4,128)S(1)} %get-tuple-element.37, bf16[4,256,4,64]{1,3,2,0:T(8,128)(2,1)S(1)} %copy-done.9, bf16[3,256,4,64]{1,3,2,0:T(8,128)(2,1)S(1)} %copy.24, bf16[1,256,4,64]{1,3,2,0:T(8,128)(2,1)S(1)} %bitcast.115), kind=kOutput, calls=%fused_computation.87 | convolution fusion | flops 276037632 | bytes 9977856 | tf_op jit(solution)/shard_map/bhqk,bkhd->bqhd/dot_general | solution.py:100
  81.7 30.6 %reduce-scatter.4.cloned.1.call-done = bf16[256,1024]{1,0:T(8,128)(2,1)} async-done(((bf16[1024,1024]{1,0:T(8,128)(2,1)}), bf16[256,1024]{1,0:T(8,128)(2,1)}) %reduce-scatter.4.cloned.1.call-update) | async-done | bytes 524304 | tf_op jit(solution)/shard_map/reduce_scatter | solution.py:158
  114.9 22.7 %all-gather.7.cloned.1.call-done = bf16[1024,1024]{1,0:T(8,128)(2,1)} async-done(((bf16[256,1024]{1,0:T(8,128)(2,1)}), bf16[1024,1024]{1,0:T(8,128)(2,1)}) %all-gather.7.cloned.1.call-update) | async-done | bytes 2097168 | tf_op jit(solution)/shard_map/all_gather | solution.py:166
  137.6 8.1 %fusion.46 = bf16[1024,1024]{1,0:T(8,128)(2,1)} fusion(bf16[1024,1024]{1,0:T(8,128)(2,1)S(1)} %copy-done, bf16[1024,1024]{1,0:T(8,128)(2,1)} %all-gather.7.cloned.1.call-done, bf16[1024,1024]{1,0:T(8,128)(2,1)} %param.17), kind=kOutput, calls=%fused_computation.62 | convolution fusion | flops 4305453056 | bytes 8388608 | tf_op jit(solution)/shard_map/dot_general | solution.py:171
  145.8 31.5 %reduce-scatter.6.cloned.1.call-done = bf16[256,1024]{1,0:T(8,128)(2,1)} async-done(((bf16[1024,1024]{1,0:T(8,128)(2,1)}), bf16[256,1024]{1,0:T(8,128)(2,1)}) %reduce-scatter.6.cloned.1.call-update) | async-done | bytes 524304 | tf_op jit(solution)/shard_map/reduce_scatter | solution.py:170
  180.1 6.2 %all_gather.17 = f32[1024,100]{0,1:T(8,128)S(1)} all-gather(f32[256,100]{0,1:T(8,128)S(1)} %fusion.70), channel_id=1, replica_groups=mesh['tm'=8,'sub'=4] {'sub'}, dimensions={0}, use_global_device_ids=true | all-gather | bytes 512000 | tf_op jit(solution)/shard_map/all_gather | solution.py:181
  186.4 3.4 collective-permute-start.2
  191.5 4.0 %collective-permute-done.3 = bf16[4,100]{0,1:T(8,128)(2,1)S(1)} collective-permute-done((bf16[4,100]{0,1:T(8,128)(2,1)S(1)}, bf16[4,100]{0,1:T(8,128)(2,1)S(1)}, u32[]{:S(2)}, u32[]{:S(2)}) %collective-permute-start.3) | collective-permute-done | bytes 832 | tf_op jit(solution)/shard_map/ppermute | solution.py:31
  209.7 7.5 %copy.35 = bf16[1024,4,768]{2,1,0:T(4,128)(2,1)} copy(bf16[1024,4,768]{2,0,1:T(8,128)(2,1)S(1)} %pad_maximum_fusion) | data formatting | bytes 12582912 | tf_op jit(solution)/shard_map/stack | solution.py:64
  217.2 10.8 %convert_element_type.108 = bf16[4096,768]{1,0:T(8,128)(2,1)} reshape(bf16[1024,4,768]{2,1,0:T(4,128)(2,1)} %copy.35) | data formatting | bytes 12582912 | tf_op jit(solution)/shard_map/convert_element_type | solution.py:200
  229.3 57.5 %reduce-scatter.8.cloned.1.call-done = bf16[1024,768]{1,0:T(8,128)(2,1)} async-done(((bf16[4096,768]{1,0:T(8,128)(2,1)}), bf16[1024,768]{1,0:T(8,128)(2,1)}) %reduce-scatter.8.cloned.1.call-update) | async-done | bytes 1572880 | tf_op jit(solution)/shard_map/reduce_scatter | solution.py:197
  292.4 7.7 %concatenate.35 = bf16[1032,768]{1,0:T(8,128)(2,1)S(1)} concatenate(bf16[4,768]{1,0:T(4,128)(2,1)S(1)} %collective-permute-done.4, bf16[1024,768]{1,0:T(8,128)(2,1)} %reduce-scatter.8.cloned.1.call-done, bf16[4,768]{1,0:T(4,128)(2,1)S(1)} %collective-permute-done.5), dimensions={0} | concatenate | bytes 3170304 | tf_op jit(solution)/shard_map/concatenate | solution.py:27
  300.1 11.6 %fusion.28 = bf16[1032,768]{1,0:T(8,128)(2,1)} fusion(bf16[1032,768]{1,0:T(8,128)(2,1)S(1)} %concatenate.35, f32[768]{0:T(1024)S(1)} %get-tuple-element.9), kind=kLoop, calls=%fused_computation.41 | loop fusion | flops 4755456 | bytes 3173376 | tf_op jit(solution)/shard_map/convert_element_type | solution.py:206
  311.8 7.3 %all-gather.9.cloned.1.call-done = bf16[3,768,768]{2,1,0:T(8,128)(2,1)} async-done(((bf16[3,192,768]{2,1,0:T(8,128)(2,1)}), bf16[3,768,768]{2,1,0:T(8,128)(2,1)}) %all-gather.9.cloned.1.call-update) | async-done | bytes 3538960 | tf_op jit(solution)/shard_map/all_gather | solution.py:107
  319.1 3.3 fusion.54
  323.9 12.8 %select_convert_fusion = bf16[1026,768]{1,0:T(8,128)(2,1)} fusion(f32[1026,768]{1,0:T(8,128)S(1)} %convolution_add_fusion.1, bf16[1032,768]{1,0:T(8,128)(2,1)S(1)} %copy-done.5, f32[768]{0:T(1024)S(1)} %get-tuple-element.8, pred[1026]{0:T(1024)(128)(4,1)S(1)} %fusion.171, bf16[3,768,768]{2,1,0:T(8,128)(2,1)S(1)} %copy-done.15), kind=kOutput, calls=%fused_computation.42 | convolution fusion | flops 1215834624 | bytes 7517184 | tf_op jit(solution)/shard_map/dot_general | solution.py:109
  336.7 14.8 %all-gather.11.cloned.1.call-done = bf16[3,768,768]{2,1,0:T(8,128)(2,1)} async-done(((bf16[3,192,768]{2,1,0:T(8,128)(2,1)}), bf16[3,768,768]{2,1,0:T(8,128)(2,1)}) %all-gather.11.cloned.1.call-update) | async-done | bytes 3538960 | tf_op jit(solution)/shard_map/all_gather | solution.py:120
  351.6 3.3 fusion.57
  356.8 2.8 add_convert_fusion
  (116 shorter events, 58.7 us)
Async XLA Ops:
  7.2 130.4 %copy-start = (bf16[1024,1024]{1,0:T(8,128)(2,1)S(1)}, bf16[1024,1024]{1,0:T(8,128)(2,1)}, u32[]{:S(2)}) copy-start(bf16[1024,1024]{1,0:T(8,128)(2,1)} %param.18) | copy-start | bytes 6291460
  7.2 27.7 %all-gather.5.cloned.1.call-start = ((), (), s32[]{:S(2)}) async-start(), calls=%async_computation.3 | async-start | bytes 2621440 | tf_op jit(solution)/shard_map/all_gather | solution.py:148
  7.9 104.4 %reduce-scatter.4.cloned.1.call-start = ((), (), s32[]{:S(2)}) async-start(), calls=%async_computation.4 | async-start | bytes 2621440 | tf_op jit(solution)/shard_map/reduce_scatter | solution.py:158
  49.7 15.9 %collective-permute-start.1 = (bf16[256,256]{1,0:T(8,128)(2,1)}, bf16[256,256]{1,0:T(8,128)(2,1)}, u32[]{:S(2)}, u32[]{:S(2)}) collective-permute-start(bf16[256,256]{1,0:T(8,128)(2,1)} %get-tuple-element.15), channel_id=1, source_target_pairs={{0,4},{4,8},{8,12},{12,16},{16,20},{20,24},{24,28},{1,5},{5,9},{9,... | collective-permute-start | bytes 393224 | tf_op jit(solution)/shard_map/ppermute | solution.py:18
  62.6 11.4 %collective-permute-start = (bf16[256,256]{1,0:T(8,128)(2,1)}, bf16[256,256]{1,0:T(8,128)(2,1)S(1)}, u32[]{:S(2)}, u32[]{:S(2)}) collective-permute-start(bf16[256,256]{1,0:T(8,128)(2,1)} %get-tuple-element.14), channel_id=1, source_target_pairs={{0,4},{4,8},{8,12},{12,16},{16,20},{20,24},{24,28},{1,5},{5,9},{9,... | collective-permute-start | bytes 393224 | tf_op jit(solution)/shard_map/ppermute | solution.py:18
  66.5 7.5 %copy-start.9 = (bf16[4,256,4,64]{1,3,2,0:T(8,128)(2,1)S(1)}, bf16[4,256,4,64]{1,3,2,0:T(8,128)(2,1)}, u32[]{:S(2)}) copy-start(bf16[4,256,4,64]{1,3,2,0:T(8,128)(2,1)} %copy.26) | copy-start | bytes 1572868
  74.1 5.5 %copy-start.10 = (bf16[256,1024]{1,0:T(8,128)(2,1)S(1)}, bf16[256,1024]{1,0:T(8,128)(2,1)}, u32[]{:S(2)}) copy-start(bf16[256,1024]{1,0:T(8,128)(2,1)} %param.16) | copy-start | bytes 1572868
  79.4 32.9 %copy-start.4 = (bf16[256,1024]{1,0:T(8,128)(2,1)S(1)}, bf16[256,1024]{1,0:T(8,128)(2,1)}, u32[]{:S(2)}) copy-start(bf16[256,1024]{1,0:T(8,128)(2,1)} %param.13) | copy-start | bytes 1572868
  81.7 55.9 %all-gather.7.cloned.1.call-start = ((), (), s32[]{:S(2)}) async-start(), calls=%async_computation.5 | async-start | bytes 2621440 | tf_op jit(solution)/shard_map/all_gather | solution.py:166
  114.8 62.5 %reduce-scatter.6.cloned.1.call-start = ((), (), s32[]{:S(2)}) async-start(), calls=%async_computation.6 | async-start | bytes 2621440 | tf_op jit(solution)/shard_map/reduce_scatter | solution.py:170
  145.7 33.0 %copy-start.13 = (f32[1,1024]{1,0:T(1,128)S(1)}, f32[1,1024]{1,0:T(1,128)}, u32[]{:S(2)}) copy-start(f32[1,1024]{1,0:T(1,128)} %get-tuple-element.23) | copy-start | bytes 12292
  145.7 33.0 %copy-start.14 = (f32[1,1024]{1,0:T(1,128)S(1)}, f32[1,1024]{1,0:T(1,128)}, u32[]{:S(2)}) copy-start(f32[1,1024]{1,0:T(1,128)} %get-tuple-element.30) | copy-start | bytes 12292
  145.7 33.0 %copy-start.16 = (bf16[1024,100]{0,1:T(8,128)(2,1)S(1)}, bf16[1024,100]{0,1:T(8,128)(2,1)}, u32[]{:S(2)}) copy-start(bf16[1024,100]{0,1:T(8,128)(2,1)} %param.19) | copy-start | bytes 614404
  145.7 50.1 %copy-start.8 = (bf16[7,384,100]{1,2,0:T(8,128)(2,1)S(1)}, bf16[7,384,100]{1,2,0:T(8,128)(2,1)}, u32[]{:S(2)}) copy-start(bf16[7,384,100]{1,2,0:T(8,128)(2,1)} %param.21) | copy-start | bytes 1612804
  145.7 141.1 %reduce-scatter.8.cloned.1.call-start = ((), (), s32[]{:S(2)}) async-start(), calls=%async_computation.7 | async-start | bytes 7864320 | tf_op jit(solution)/shard_map/reduce_scatter | solution.py:197
  186.4 5.1 %collective-permute-start.2 = (bf16[4,100]{0,1:T(8,128)(2,1)S(1)}, bf16[4,100]{0,1:T(8,128)(2,1)S(1)}, u32[]{:S(2)}, u32[]{:S(2)}) collective-permute-start(bf16[4,100]{0,1:T(8,128)(2,1)S(1)} %get-tuple-element.21), channel_id=1, source_target_pairs={{0,4},{4,8},{8,12},{12,16},{16,20},{20,24},{24,28},{1,5},{5,9},{9,... | collective-permute-start | bytes 2408 | tf_op jit(solution)/shard_map/ppermute | solution.py:29
  189.8 5.7 %collective-permute-start.3 = (bf16[4,100]{0,1:T(8,128)(2,1)S(1)}, bf16[4,100]{0,1:T(8,128)(2,1)S(1)}, u32[]{:S(2)}, u32[]{:S(2)}) collective-permute-start(bf16[4,100]{0,1:T(8,128)(2,1)S(1)} %get-tuple-element.22), channel_id=1, source_target_pairs={{4,0},{8,4},{12,8},{16,12},{20,16},{24,20},{28,24},{5,1},{9,5},{13... | collective-permute-start | bytes 2408 | tf_op jit(solution)/shard_map/ppermute | solution.py:31
  227.9 91.2 %all-gather.9.cloned.1.call-start = ((), (), s32[]{:S(2)}) async-start(), calls=%async_computation.8 | async-start | bytes 4423680 | tf_op jit(solution)/shard_map/all_gather | solution.py:107
  228.5 123.0 %all-gather.11.cloned.1.call-start = ((), (), s32[]{:S(2)}) async-start(), calls=%async_computation.9 | async-start | bytes 4423680 | tf_op jit(solution)/shard_map/all_gather | solution.py:120
  287.5 3.1 collective-permute-start.4
  289.3 3.2 collective-permute-start.5
  311.8 10.7 %copy-start.5 = (bf16[1032,768]{1,0:T(8,128)(2,1)S(1)}, bf16[1032,768]{1,0:T(8,128)(2,1)}, u32[]{:S(2)}) copy-start(bf16[1032,768]{1,0:T(8,128)(2,1)} %fusion.28) | copy-start | bytes 4755460
  336.7 18.2 %copy-start.6 = (bf16[1026,768]{1,0:T(8,128)(2,1)S(1)}, bf16[1026,768]{1,0:T(8,128)(2,1)}, u32[]{:S(2)}) copy-start(bf16[1026,768]{1,0:T(8,128)(2,1)} %select_convert_fusion) | copy-start | bytes 4727812
  356.8 3.5 copy-start.1
  (8 other events, 17.0 us)
Sparse Core Ops, SparseCore 0:
  9.6 25.2 all-gather.4
  81.8 30.4 reduce-scatter.3
  114.9 22.5 all-gather.6
  145.8 31.4 reduce-scatter.5
  228.1 58.7 reduce-scatter.7
  288.3 30.7 all-gather.8
  320.7 30.7 all-gather.10
where the time goes:
time: 375 us; the launch traced here: 367 us
  waiting for transfers between devices  197 us (53%)
  matrix products  65.2 us (17%)
  local copies, waits for them, and re-layouts  47.9 us (13%)
  other arithmetic  21.1 us (6%)
  starting transfers between devices  15.3 us (4%)
  between operations  14.8 us (4%)
  blocking collectives  6.24 us (2%)
    reduce_scatter x1, waiting for transfers between devices, body(): lax.psum_scatter(phase_terms(prelude, w_upsample, jnp.int32(0) // 4, samp...  57.5 us
    reduce_scatter x1, waiting for transfers between devices, body(): lax.psum_scatter(jnp.dot(hidden, w_down, preferred_element_type=jnp.float...  31.5 us
    reduce_scatter x1, waiting for transfers between devices, body(): lax.psum_scatter(jnp.dot(heads_out, w_heads_out, preferred_element_type=j...  30.6 us
    all_gather x1, waiting for transfers between devices, body(): gathered = lax.all_gather(frames, 'sub', axis=0, tiled=True)  24.4 us
    all_gather x1, waiting for transfers between devices, body(): second_norm = lax.all_gather(own_norm, 'sub', axis=0, tiled=True)  22.7 us
    dot_general x3, matrix products, dilated_conv(): jnp.dot(extended[3 * offset:3 * offset + row_count], weight_rows[offset],...  17.6 us
    all_gather x1, waiting for transfers between devices, plain_conv(): weight_rows = lax.all_gather(w_plain, 'sub', axis=1, tiled=True)  14.8 us
    convert_element_type x1, other arithmetic, body(): snake_act(wide_up.astype(jnp.float32), snake_alpha[0]).astype(jnp.bfloat16)  11.6 us
  transfers between devices with their start and end apart: 13, of which 9 were waited for; matrix products, arithmetic and copies ran while one was open for 16% of the time, Pallas kernels for 0%

commit v1 on v0

v1 whole, which is shorter than its diff:
```python
import functools
import math

import jax
import jax.numpy as jnp
from jax import lax
from jax.experimental import pallas as pl
from jax.experimental.pallas import tpu as pltpu
from jax.sharding import PartitionSpec as P

HEAD_DIM = 64
BLK = 256
EPSILON = 1e-06
MESH = pl.DeviceIdType.MESH
VMEM = pltpu.VMEM
DMA = pltpu.SemaphoreType.DMA
F32 = jnp.float32
BF16 = jnp.bfloat16


def norm_rows(rows, offset_row, scale_row):
    center = jnp.mean(rows, axis=-1, keepdims=True)
    square = jnp.mean(rows * rows, axis=-1, keepdims=True)
    spread = square - center * center
    return (rows - center) * lax.rsqrt(spread + EPSILON) * (1.0 + scale_row) + offset_row


def sin_squared(values):
    turns = jnp.round(values * (1.0 / math.pi))
    rest = values - turns * 3.140625
    rest = rest - turns * 9.670257568359375e-04
    rest = rest - turns * 6.2783295e-07
    rest = jnp.clip(rest, -0.5 * math.pi - 1e-3, 0.5 * math.pi + 1e-3)
    u = rest * rest
    series = -1.0 / 39916800.0
    for coefficient in (1.0 / 362880.0, -1.0 / 5040.0, 1.0 / 120.0, -1.0 / 6.0, 1.0):
        series = series * u + coefficient
    return u * series * series


def snake_act(values, alpha_row):
    return values + sin_squared(alpha_row * values) * (1.0 / alpha_row)


def dot(left, right):
    return jnp.dot(left, right, preferred_element_type=F32)


def dot_t(left, right):
    return lax.dot_general(left, right, (((1,), (1,)), ((), ())), preferred_element_type=F32)


class Place:
    def __init__(self):
        self.s = lax.axis_index("sub")
        self.t = lax.axis_index("tm")
        self.n = lax.axis_size("sub")
        self.times = lax.axis_size("tm")
        self.chips = self.n // 2
        self.core = lax.rem(self.s, 2)
        self.chip = self.s // 2
        self.sibling = self.s + 1 - 2 * self.core

    def chip_behind(self, i):
        return lax.rem(self.chip + self.chips - i, self.chips)

    def block(self, i, other_core):
        core = 1 - self.core if other_core else self.core
        return self.chip_behind(i) * 2 + core

    def peer(self, chip):
        return {"sub": chip * 2 + self.core}


def remote(src, dst, send, recv, device):
    return pltpu.make_async_remote_copy(
        src_ref=src, dst_ref=dst, send_sem=send, recv_sem=recv, device_id=device, device_id_type=MESH
    )


def rows_of(block, rows):
    return pl.ds(pl.multiple_of(block * rows, rows), rows)


class Gather:
    def __init__(self, here, buf, rows, sems):
        self.here, self.buf, self.rows = here, buf, rows
        self.x_send, self.x_recv, self.d_send, self.d_recv = sems

    def piece(self, block):
        return self.buf.at[rows_of(block, self.rows)]

    def across(self, i):
        here = self.here
        ahead = lax.rem(here.chip + i, here.chips)
        own = self.piece(here.s)
        return remote(own, own, self.x_send.at[i], self.x_recv.at[i], here.peer(ahead))

    def arriving(self, i):
        own = self.piece(self.here.block(i, False))
        return remote(own, own, self.x_send.at[i], self.x_recv.at[i], self.here.peer(self.here.chip_behind(i)))

    def forward(self, i):
        own = self.piece(self.here.block(i, False))
        return remote(own, own, self.d_send.at[i], self.d_recv.at[i], {"sub": self.here.sibling})

    def start(self):
        for i in range(1, self.here.chips):
            self.across(i).start()
        self.forward(0).start()

    def finish(self):
        for i in range(1, self.here.chips):
            self.across(i).wait_send()
        for i in range(self.here.chips):
            self.forward(i).wait_send()

    def each(self, work):
        here = self.here
        work(here.block(0, False), 0, False)
        self.take_other(0)
        work(here.block(0, True), 0, True)

        def step(i, carry):
            self.arriving(i).wait_recv()
            self.forward(i).start()
            work(here.block(i, False), i, False)
            self.take_other(i)
            work(here.block(i, True), i, True)
            return carry

        lax.fori_loop(1, here.chips, step, 0)

    def take_other(self, i):
        own = self.piece(self.here.block(i, True))
        remote(own, own, self.d_send.at[i], self.d_recv.at[i], {"sub": self.here.sibling}).wait_recv()


class Scatter:
    def __init__(self, here, buf, rows, near, far, sems):
        self.here, self.buf, self.rows, self.near, self.far = here, buf, rows, near, far
        self.a_send, self.a_recv, self.b_send, self.b_recv = sems

    def piece(self, block):
        return self.buf.at[rows_of(block, self.rows)]

    def to_sibling(self, i):
        here = self.here
        return remote(
            self.piece(here.block(i, True)), self.near.at[i], self.a_send.at[i], self.a_recv.at[i],
            {"sub": here.sibling},
        )

    def to_chip(self, i):
        here = self.here
        return remote(
            self.piece(here.block(i, False)), self.far.at[i], self.b_send.at[i], self.b_recv.at[i],
            here.peer(here.chip_behind(i)),
        )

    def pass_on(self, i):
        self.to_sibling(i).wait_recv()
        here, rows = self.here, self.rows
        base = here.block(i, False) * rows
        step = min(64, rows)

        def add(q, carry):
            at = pl.ds(pl.multiple_of(base + q * step, step), step)
            near_at = pl.ds(pl.multiple_of(q * step, step), step)
            self.buf[at] = (self.buf[at].astype(F32) + self.near[i, near_at].astype(F32)).astype(BF16)
            return carry

        lax.fori_loop(0, rows // step, add, 0)
        self.to_chip(i).start()

    def arrive(self):
        self.to_sibling(0).wait_recv()
        for i in range(1, self.here.chips):
            self.to_chip(i).wait_recv()

    def total(self, at):
        start, size = at
        own = pl.ds(pl.multiple_of(self.here.s * self.rows + start, size), size)
        part = pl.ds(pl.multiple_of(start, size), size)
        total = self.buf[own].astype(F32) + self.near[0, part].astype(F32)
        for i in range(1, self.here.chips):
            total = total + self.far[i, part].astype(F32)
        return total

    def finish(self):
        for i in range(self.here.chips):
            self.to_sibling(i).wait_send()
        for i in range(1, self.here.chips):
            self.to_chip(i).wait_send()


def greet(here, extra=()):
    barrier = pltpu.get_barrier_semaphore()
    for i in range(1, here.chips):
        ahead = lax.rem(here.chip + i, here.chips)
        pl.semaphore_signal(barrier, inc=1, device_id=here.peer(ahead), device_id_type=MESH)
    pl.semaphore_signal(barrier, inc=1, device_id={"sub": here.sibling}, device_id_type=MESH)
    for condition, device in extra:

        @pl.when(condition)
        def _():
            pl.semaphore_signal(barrier, inc=1, device_id=device, device_id_type=MESH)

    greeted = here.chips
    for condition, device in extra:
        greeted = greeted + condition.astype(jnp.int32)
    pl.semaphore_wait(barrier, greeted)


def layer_kernel(
    frames, mod, w_project, w_heads_out, w_up, w_down, w_velocity, noisy, mel_out,
    h_one, h_two, queries, keys, values, attended, sums_one, sums_two, near_one, far_one, near_two,
    far_two, mixed, mel_all, gather_sems, scatter_sems, look_send, look_recv,
):
    here = Place()
    rows, width = frames.shape
    total_rows = here.n * rows
    step = min(64, rows)
    steps = rows // step
    first, last = here.t == 0, here.t == here.times - 1
    behind, ahead = {"tm": here.t - 1}, {"tm": here.t + 1}
    greet(here, ((here.t > 0, behind), (here.t < here.times - 1, ahead)))

    def at_step(q, base=0):
        return pl.ds(pl.multiple_of(base + q * step, step), step)

    def norm_one(q, carry):
        out = norm_rows(frames[at_step(q)].astype(F32), mod[0:1], mod[1:2])
        h_one[at_step(q, here.s * rows)] = out.astype(BF16)
        return carry

    lax.fori_loop(0, steps, norm_one, 0)
    gather = Gather(here, h_one, rows, [gather_sems.at[0, j] for j in range(4)])
    gather.start()

    def project(block, i, other):
        at = rows_of(block, rows)
        later = pl.ds(pl.multiple_of(BLK + block * rows, math.gcd(BLK, rows)), rows)
        h = h_one[at]
        queries[at] = (dot(h, w_project[0]).astype(BF16).astype(F32) * (1.0 / math.sqrt(HEAD_DIM))).astype(BF16)
        keys[later] = dot(h, w_project[1]).astype(BF16)
        values[later] = dot(h, w_project[2]).astype(BF16)

    gather.each(project)

    def lookback(buf, j):
        return remote(
            buf.at[pl.ds(total_rows, BLK)], buf.at[pl.ds(0, BLK)], look_send.at[j], look_recv.at[j], ahead
        )

    @pl.when(jnp.logical_not(last))
    def _():
        lookback(keys, 0).start()
        lookback(values, 1).start()

    @pl.when(first)
    def _():
        keys[pl.ds(0, BLK)] = jnp.zeros((BLK, keys.shape[1]), BF16)
        values[pl.ds(0, BLK)] = jnp.zeros((BLK, values.shape[1]), BF16)

    blocks = total_rows // BLK
    heads = queries.shape[1] // HEAD_DIM

    def attend(turn, carry):
        b = lax.rem(turn + 1, blocks)

        @pl.when(jnp.logical_and(b == 0, jnp.logical_not(first)))
        def _():
            lookback(keys, 0).wait_recv()
            lookback(values, 1).wait_recv()

        at = rows_of(b, BLK)
        both = pl.ds(pl.multiple_of(b * BLK, BLK), 2 * BLK)
        key_ids = lax.broadcasted_iota(jnp.int32, (1, 2 * BLK), 1)
        hidden_keys = jnp.where((key_ids < BLK) & (b == 0) & first, -1e30, 0.0)
        for head in range(heads):
            cols = slice(head * HEAD_DIM, (head + 1) * HEAD_DIM)
            scores = dot_t(queries[at, cols], keys[both, cols]) + hidden_keys
            raised = jnp.exp(scores - jnp.max(scores, axis=-1, keepdims=True))
            scale = 1.0 / jnp.sum(raised, axis=-1, keepdims=True)
            attended[:, cols] = (dot(raised.astype(BF16), values[both, cols]) * scale).astype(BF16)
        sums_one[at] = dot(attended[...], w_heads_out[...]).astype(BF16)
        return carry

    lax.fori_loop(0, blocks, attend, 0)

    scatter = Scatter(here, sums_one, rows, near_one, far_one, [scatter_sems.at[0, j] for j in range(4)])
    for i in reversed(range(here.chips)):
        scatter.to_sibling(i).start()
    for i in range(1, here.chips):
        scatter.pass_on(i)
    scatter.arrive()

    def norm_two(q, carry):
        attn = scatter.total((q * step, step))
        mix = (frames[at_step(q)].astype(F32) + mod[2:3] * attn).astype(BF16)
        mixed[at_step(q)] = mix
        h_two[at_step(q, here.s * rows)] = norm_rows(mix.astype(F32), mod[3:4], mod[4:5]).astype(BF16)
        return carry

    lax.fori_loop(0, steps, norm_two, 0)
    gather_two = Gather(here, h_two, rows, [gather_sems.at[1, j] for j in range(4)])
    gather_two.start()
    scatter_two = Scatter(here, sums_two, rows, near_two, far_two, [scatter_sems.at[1, j] for j in range(4)])

    def feed_forward(block, i, other):
        at = rows_of(block, rows)
        hidden = jax.nn.gelu(dot(h_two[at], w_up[...]), approximate=True).astype(BF16)
        sums_two[at] = dot(hidden, w_down[...]).astype(BF16)
        if other:
            scatter_two.to_sibling(i).start()

    gather_two.each(feed_forward)
    for i in range(1, here.chips):
        scatter_two.pass_on(i)
    scatter_two.arrive()

    def step_mel(q, carry):
        feed = scatter_two.total((q * step, step))
        final = (mixed[at_step(q)].astype(F32) + mod[5:6] * feed).astype(BF16)
        normed = norm_rows(final.astype(F32), mod[6:7], mod[7:8]).astype(BF16)
        own = at_step(q, here.s * rows)
        mel_all[own] = noisy[own] + 0.5 * dot(normed, w_velocity[...])
        return carry

    lax.fori_loop(0, steps, step_mel, 0)
    gather_mel = Gather(here, mel_all, rows, [gather_sems.at[2, j] for j in range(4)])
    gather_mel.start()

    def hand_out(block, i, other):
        mel_out[rows_of(block, rows)] = mel_all[rows_of(block, rows)]

    gather_mel.each(hand_out)

    @pl.when(jnp.logical_not(last))
    def _():
        lookback(keys, 0).wait_send()
        lookback(values, 1).wait_send()

    for one in (gather, gather_two, gather_mel, scatter, scatter_two):
        one.finish()


def layer(frames, modulation, w_project, w_heads_out, w_up, w_down, w_velocity, noisy_mel):
    n = lax.axis_size("sub")
    rows, width = frames.shape
    total_rows = n * rows
    cols = w_project.shape[2]
    mel = noisy_mel.shape[1]
    chips = n // 2
    return pl.pallas_call(
        layer_kernel,
        out_shape=jax.ShapeDtypeStruct((total_rows, mel), F32),
        in_specs=[pl.BlockSpec(memory_space=VMEM)] * 8,
        out_specs=pl.BlockSpec(memory_space=VMEM),
        scratch_shapes=[
            VMEM((total_rows, width), BF16),
            VMEM((total_rows, width), BF16),
            VMEM((total_rows, cols), BF16),
            VMEM((total_rows + BLK, cols), BF16),
            VMEM((total_rows + BLK, cols), BF16),
            VMEM((BLK, cols), BF16),
            VMEM((total_rows, width), BF16),
            VMEM((total_rows, width), BF16),
            VMEM((chips, rows, width), BF16),
            VMEM((chips, rows, width), BF16),
            VMEM((chips, rows, width), BF16),
            VMEM((chips, rows, width), BF16),
            VMEM((rows, width), BF16),
            VMEM((total_rows, mel), F32),
            DMA((3, 4, chips)),
            DMA((2, 4, chips)),
            DMA((2,)),
            DMA((2,)),
        ],
        compiler_params=pltpu.CompilerParams(
            collective_id=0, has_side_effects=True, vmem_limit_bytes=48 * 2**20
        ),
        cost_estimate=pl.CostEstimate(flops=80 * 10**9, bytes_accessed=8 * 2**20, transcendentals=0),
        name="layer",
    )(frames, modulation, w_project, w_heads_out, w_up, w_down, w_velocity, noisy_mel)


def section_kernel(
    mel, w_prelude, w_upsample, alpha, w_dilated, w_plain, out,
    mel_wide, prelude, sums, near, far, up, taps, acts, woven, halo_low, halo_high,
    scatter_sems, edge_send, edge_recv,
):
    here = Place()
    total_rows, bands = mel.shape
    rows = total_rows // here.n
    mid = w_upsample.shape[2]
    s, t = here.s, here.t
    first, last = t == 0, t == here.times - 1
    begin, end = first & (s == 0), last & (s == here.n - 1)
    not_first, not_last = t > 0, t < here.times - 1
    behind, ahead = {"tm": t - 1}, {"tm": t + 1}
    spot = t * here.n + s
    low_spot, high_spot = spot - 1, spot + 1
    earlier = {"tm": low_spot // here.n, "sub": lax.rem(low_spot, here.n)}
    later = {"tm": high_spot // here.n, "sub": lax.rem(high_spot, here.n)}
    not_begin, not_end = spot > 0, spot < here.times * here.n - 1
    greet(here, ((not_first, behind), (not_last, ahead), (not_begin, earlier), (not_end, later)))

    zeros16 = jnp.zeros((16, bands), F32)

    mel_wide[pl.ds(0, 8)] = zeros16[:8]
    mel_wide[pl.ds(total_rows + 24, 8)] = zeros16[:8]

    @pl.when(first)
    def _():
        mel_wide[pl.ds(8, 8)] = zeros16[:8]

    @pl.when(last)
    def _():
        mel_wide[pl.ds(total_rows + 16, 8)] = zeros16[:8]

    mel_wide[pl.ds(16, total_rows)] = mel[...]
    mel_up = remote(
        mel_wide.at[pl.ds(total_rows + 8, 8)], mel_wide.at[pl.ds(8, 8)], edge_send.at[0], edge_recv.at[0], ahead
    )
    mel_down = remote(
        mel_wide.at[pl.ds(16, 8)], mel_wide.at[pl.ds(total_rows + 16, 8)], edge_send.at[1], edge_recv.at[1], behind
    )

    @pl.when(not_last)
    def _():
        mel_up.start()

    @pl.when(not_first)
    def _():
        mel_down.start()

    def prelude_rows(start, count):
        wide = mel_wide[pl.ds(start, count + 16)]
        total = jnp.zeros((count, w_prelude.shape[1]), F32)
        for j in range(w_prelude.shape[0]):
            total = total + dot_t(wide[5 + j : 5 + j + count].astype(BF16), w_prelude[j])
        return total.astype(BF16).astype(F32)

    @pl.when(not_first)
    def _():
        mel_up.wait_recv()

    @pl.when(not_last)
    def _():
        mel_down.wait_recv()

    def prelude_step(q, carry):
        base = pl.multiple_of(q * rows + 8, 8)
        prelude[pl.ds(base, rows)] = prelude_rows(base, rows)
        return carry

    lax.fori_loop(0, here.n, prelude_step, 0)
    prelude[pl.ds(0, 8)] = jnp.where(not_first, prelude_rows(0, 8), 0.0)
    prelude[pl.ds(total_rows + 8, 8)] = jnp.where(not_last, prelude_rows(total_rows + 8, 8), 0.0)

    scatter = Scatter(here, sums, rows, near, far, [scatter_sems.at[j] for j in range(4)])

    def upsample(block):
        wide = prelude[pl.ds(pl.multiple_of(block * rows, rows), rows + 16)]
        before = wide[7 : 7 + rows].astype(BF16)
        now = wide[8 : 8 + rows].astype(BF16)
        after = wide[9 : 9 + rows].astype(BF16)
        at = rows_of(block, rows)
        for phase in range(4):
            other, tap = (before, phase + 6) if phase < 2 else (after, phase - 2)
            result = dot(now, w_upsample[phase + 2]) + dot(other, w_upsample[tap])
            sums[at, phase * mid : (phase + 1) * mid] = result.astype(BF16)

    def upsample_step(p, carry):
        i = here.chips - 1 - p
        upsample(here.block(i, True))
        scatter.to_sibling(i).start()
        upsample(here.block(i, False))

        @pl.when(i > 0)
        def _():
            scatter.pass_on(i)

        return carry

    lax.fori_loop(0, here.chips, upsample_step, 0)
    scatter.arrive()

    step = min(64, rows)

    def total_step(q, carry):
        start = q * step
        up[pl.ds(pl.multiple_of(16 + start, 16), step)] = scatter.total((start, step)).astype(BF16)
        return carry

    lax.fori_loop(0, rows // step, total_step, 0)

    up_send = remote(up.at[pl.ds(rows, 16)], halo_low, edge_send.at[2], edge_recv.at[2], later)
    down_send = remote(up.at[pl.ds(16, 16)], halo_high, edge_send.at[3], edge_recv.at[3], earlier)

    @pl.when(not_end)
    def _():
        up_send.start()

    @pl.when(not_begin)
    def _():
        down_send.start()

    @pl.when(begin)
    def _():
        halo_low[...] = jnp.zeros(halo_low.shape, BF16)

    @pl.when(end)
    def _():
        halo_high[...] = jnp.zeros(halo_high.shape, BF16)

    alpha_one, alpha_two = alpha[0:1], alpha[1:2]

    def act_step(q, carry):
        start = q * step
        source = pl.ds(pl.multiple_of(16 + start, 16), step)
        target = pl.ds(pl.multiple_of(8 + start, 8), step)
        for phase in range(4):
            block = up[source, phase * mid : (phase + 1) * mid].astype(F32)
            acts[phase, target] = snake_act(block, alpha_one)
        return carry

    lax.fori_loop(0, rows // step, act_step, 0)

    @pl.when(not_begin)
    def _():
        up_send.wait_recv()

    @pl.when(not_end)
    def _():
        down_send.wait_recv()

    for phase in range(4):
        cols = slice(phase * mid, (phase + 1) * mid)
        acts[phase, pl.ds(0, 8)] = snake_act(halo_low[:, cols].astype(F32)[8:16], alpha_one)
        acts[phase, pl.ds(rows + 8, 8)] = snake_act(halo_high[:, cols].astype(F32)[0:8], alpha_one)

    length = rows + 16

    def prepare(befores, afters):
        for phase in range(4):
            block = acts[phase]
            taps[phase] = block.astype(BF16)
            if phase in befores:
                taps[4 + befores.index(phase)] = pltpu.roll(block, 1, 0).astype(BF16)
            if phase in afters:
                taps[4 + len(befores) + afters.index(phase)] = pltpu.roll(block, length - 1, 0).astype(BF16)

    chunk = 256 if mid % 256 == 0 else mid
    prepare((1, 2, 3), (0, 1, 2))
    line = lax.broadcasted_iota(jnp.int32, (length, 1), 0)
    outside = (begin & (line < 8)) | (end & (line >= rows + 8))
    row_mask = jnp.where(outside, 0.0, 1.0)

    def dilated_step(q, carry):
        cols = pl.ds(pl.multiple_of(q * chunk, chunk), chunk)
        row = alpha[1:2, cols]
        for phase in range(4):
            low = 4 + phase if phase < 3 else 0
            high = 3 if phase == 0 else 6 + phase
            inner = dot(taps[low], w_dilated[0, :, cols])
            inner = inner + dot(taps[phase], w_dilated[1, :, cols])
            inner = inner + dot(taps[high], w_dilated[2, :, cols])
            acts[phase, :, cols] = snake_act(inner, row) * row_mask
        return carry

    lax.fori_loop(0, mid // chunk, dilated_step, 0)
    prepare((3,), (0,))

    def plain_step(q, carry):
        cols = pl.ds(pl.multiple_of(q * chunk, chunk), chunk)
        for phase in range(4):
            low = 4 if phase == 0 else phase - 1
            high = 5 if phase == 3 else phase + 1
            outer = dot(taps[low], w_plain[0, :, cols])
            outer = outer + dot(taps[phase], w_plain[1, :, cols])
            outer = outer + dot(taps[high], w_plain[2, :, cols])
            base = up[pl.ds(16, rows), pl.ds(pl.multiple_of(phase * mid + q * chunk, chunk), chunk)]
            result = base.astype(F32) + outer[8 : 8 + rows]
            for lane in range(chunk // 128):
                woven[phase, :, pl.ds(pl.multiple_of(q * chunk + lane * 128, 128), 128)] = result[
                    :, lane * 128 : (lane + 1) * 128
                ]
        return carry

    lax.fori_loop(0, mid // chunk, plain_step, 0)

    def weave_step(q, carry):
        part = [woven[phase, pl.ds(pl.multiple_of(q * 16, 16), 16)] for phase in range(4)]
        out[pl.ds(pl.multiple_of(q * 64, 64), 64)] = jnp.stack(part, 1).reshape(64, mid).astype(BF16)
        return carry

    lax.fori_loop(0, rows // 16, weave_step, 0)

    @pl.when(not_last)
    def _():
        mel_up.wait_send()

    @pl.when(not_first)
    def _():
        mel_down.wait_send()

    @pl.when(not_end)
    def _():
        up_send.wait_send()

    @pl.when(not_begin)
    def _():
        down_send.wait_send()

    scatter.finish()


def section(mel, w_prelude, w_upsample, snake_alpha, w_dilated, w_plain):
    n = lax.axis_size("sub")
    chips = n // 2
    total_rows, bands = mel.shape
    rows = total_rows // n
    mid = w_upsample.shape[2]
    wide = 4 * mid
    return pl.pallas_call(
        section_kernel,
        out_shape=jax.ShapeDtypeStruct((4 * rows, mid), BF16),
        in_specs=[pl.BlockSpec(memory_space=VMEM)] * 6,
        out_specs=pl.BlockSpec(memory_space=VMEM),
        scratch_shapes=[
            VMEM((total_rows + 32, bands), F32),
            VMEM((total_rows + 16, w_prelude.shape[1]), F32),
            VMEM((total_rows, wide), BF16),
            VMEM((chips, rows, wide), BF16),
            VMEM((chips, rows, wide), BF16),
            VMEM((rows + 16, wide), BF16),
            VMEM((10, rows + 16, mid), BF16),
            VMEM((4, rows + 16, mid), F32),
            VMEM((4, rows, mid), F32),
            VMEM((16, wide), BF16),
            VMEM((16, wide), BF16),
            DMA((4, chips)),
            DMA((4,)),
            DMA((4,)),
        ],
        compiler_params=pltpu.CompilerParams(
            collective_id=1, has_side_effects=True, vmem_limit_bytes=58 * 2**20
        ),
        cost_estimate=pl.CostEstimate(flops=60 * 10**9, bytes_accessed=16 * 2**20, transcendentals=0),
        name="section",
    )(mel, w_prelude, w_upsample, snake_alpha, w_dilated, w_plain)


def body(
    frames, modulation, w_project, w_heads_out, w_up, w_down, w_velocity, noisy_mel, w_prelude,
    w_upsample, snake_alpha, w_dilated, w_plain,
):
    dilated_all = lax.all_gather(w_dilated, "sub", axis=1, tiled=True)
    plain_all = lax.all_gather(w_plain, "sub", axis=1, tiled=True)
    mel_next = layer(frames, modulation, w_project, w_heads_out, w_up, w_down, w_velocity, noisy_mel)
    section_out = section(mel_next, w_prelude, w_upsample, snake_alpha, dilated_all, plain_all)
    return (mel_next, section_out)


def solution(mesh):
    in_specs = (
        P(("tm", "sub"), None),
        P(),
        P(None, None, "sub"),
        P("sub", None),
        P(None, "sub"),
        P("sub", None),
        P(),
        P("tm", None),
        P(None, "sub", None),
        P(None, "sub", None),
        P(),
        P(None, "sub", None),
        P(None, "sub", None),
    )
    out_specs = (P("tm", None), P(("tm", "sub"), None))
    return jax.shard_map(body, mesh=mesh, in_specs=in_specs, out_specs=out_specs, check_vma=False)
```

time: 375 us -> 211 us (0.56); the launches traced: 367 us -> 210 us
  waiting for transfers between devices: 197 us -> 1.38 us
  Pallas kernels: 0 us -> 184 us
  matrix products: 65.2 us -> 0 us
  local copies, waits for them, and re-layouts: 47.9 us -> 10.7 us
  other arithmetic: 21.1 us -> 0 us
  starting transfers between devices: 15.3 us -> 0.08 us
  blocking collectives: 6.24 us -> 0 us
    pallas_call x0 -> x2, Pallas kernels: none -> 184 us  [the longest x1 108 us: layer(): pl.pallas_call(layer_kernel, out_shape=jax.ShapeDtypeStruct((total_rows,...]
    reduce_scatter x3 -> x0, waiting for transfers between devices: 120 us -> none  [the longest x1 57.5 us: body(): lax.psum_scatter(phase_terms(prelude, w_upsample, jnp.int32(0) // 4, samp...]
    all_gather x4 -> x2, waiting for transfers between devices: 69.3 us -> 0.01 us  [the longest x1 0.01 us: body(): dilated_all = lax.all_gather(w_dilated, 'sub', axis=1, tiled=True)]
    dot_general x26 -> x0, matrix products: 57.8 us -> none  [the longest x3 17.6 us: dilated_conv(): jnp.dot(extended[3 * offset:3 * offset + row_count], weight_rows[offset],...]
    another operation x6 -> x0, local copies, waits for them, and re-layouts: 16.7 us -> none  [the longest x1 7.46 us: phase_terms(): jnp.stack([tap_product(current, 2) + tap_product(earlier, 6), tap_product...]
    ppermute x6 -> x0, starting transfers between devices: 15 us -> none  [the longest x2 6.95 us: from_behind(): return lax.ppermute(block, axis, route)]
    convert_element_type x3 -> x0, other arithmetic: 12.7 us -> none  [the longest x1 11.6 us: body(): snake_act(wide_up.astype(jnp.float32), snake_alpha[0]).astype(jnp.bfloat16)]
    convert_element_type x2 -> x0, local copies, waits for them, and re-layouts: 11.2 us -> none  [the longest x1 10.8 us: body(): up_x = lax.psum_scatter(phase_terms(prelude, w_upsample, jnp.int32(0) //...]
  transfers between devices with their start and end apart: 13 -> 2, of which waited for: 9 -> 0; matrix products, arithmetic and copies ran while one was open for 16% -> 2% of each run, Pallas kernels for 0% -> 52%
where the time goes in v1:
time: 211 us; the launch traced here: 210 us
  Pallas kernels  184 us (87%)
  between operations  14.1 us (7%)
  local copies, waits for them, and re-layouts  10.7 us (5%)
    pallas_call x1, Pallas kernels, layer(): pl.pallas_call(layer_kernel, out_shape=jax.ShapeDtypeStruct((total_rows,...  108 us
    pallas_call x1, Pallas kernels, section(): pl.pallas_call(section_kernel, out_shape=jax.ShapeDtypeStruct((4 * rows,...  75.3 us
    unnamed x19, local copies, waits for them, and re-layouts  10.7 us
  transfers between devices with their start and end apart: 2, of which 0 were waited for; matrix products, arithmetic and copies ran while one was open for 2% of the time, Pallas kernels for 52%

profile of v1, /device:TPU:0, one launch (start us, length us, event | category | flops | bytes accessed | tf_op | source)
XLA Modules:
  0.0 210.0 jit_solution(16988986009832740066)
XLA Ops:
  7.2 0.0 copy-start.6
  7.2 0.0 copy-start.5
  7.2 0.0 copy-start.1
  7.2 0.0 all-gather.3.cloned.1.call-start
  7.2 0.7 all-gather.3.cloned.1.call-update
  7.9 0.0 all-gather.5.cloned.1.call-start
  8.0 0.7 all-gather.5.cloned.1.call-update
  8.7 1.2 copy.16.noisy
  9.9 0.0 copy-done.6
  9.9 0.2 copy.15.w_velocity
  10.1 2.2 %copy.17.w_prelude = bf16[7,384,100]{2,1,0:T(8,128)(2,1)} copy(bf16[7,384,100]{1,2,0:T(8,128)(2,1)} %param.21) | data formatting | bytes 1075200 | tf_op args[8]
  12.3 0.0 copy-done.5
  12.3 0.0 copy-done.1
  12.3 0.0 copy-start.2
  12.3 1.4 copy-done.2
  13.7 0.0 copy-start.3
  13.7 1.0 copy-done.3
  14.8 1.0 copy-done.4
  15.8 108.5 %layer.1.mel = f32[1024,100]{1,0:T(8,128)S(1)} custom-call(bf16[256,1024]{1,0:T(8,128)(2,1)S(1)} %copy-done.3, f32[8,1024]{1,0:T(8,128)S(1)} %copy-done.5, bf16[3,1024,256]{2,1,0:T(8,128)(2,1)S(1)} %copy-done.2, bf16[256,1024]{1,0:T(8,128)(2,1)S(1)} %copy-done.4, bf16[1024,1024]{1,0:T(8,128)(2,1)S(1)} %copy-done.1, bf16[1024,1024]{1,0:T(8,128)(2,1)} %w_down.1, ...), custom_call_target="tpu_custom_call" | custom-call | flops 80000000000 | bytes 8388608 | tf_op jit(solution)/shard_map/layer/pallas_call | solution.py:356
  124.3 0.0 copy-start
  124.3 1.0 copy.18
  125.3 0.0 copy-done
  125.3 75.3 %section.1 = bf16[1024,768]{1,0:T(8,128)(2,1)} custom-call(f32[1024,100]{1,0:T(8,128)} %copy-done, bf16[7,384,100]{2,1,0:T(8,128)(2,1)} %copy.17.w_prelude, bf16[8,384,768]{2,1,0:T(8,128)(2,1)} %w_upsample.1, f32[2,768]{1,0:T(2,128)} %alpha.1, bf16[3,768,768]{2,1,0:T(8,128)(2,1)} %all-gather.3.cloned.1.call-done.w_dilated, ...), custom_call_target="tpu_custom_call" | custom-call | flops 60000002048 | bytes 16777216 | tf_op jit(solution)/shard_map/section/pallas_call | solution.py:628
  200.5 2.7 %copy.20 = bf16[1024,768]{1,0:T(8,128)(2,1)} copy(bf16[1024,768]{1,0:T(8,128)(2,1)} %section.1) | data formatting | bytes 3145728
  (3 shorter events, 0.0 us)
Async XLA Ops:
  7.2 2.7 %copy-start.6 = (bf16[1024,100]{0,1:T(8,128)(2,1)S(1)}, bf16[1024,100]{0,1:T(8,128)(2,1)}, u32[]{:S(2)}) copy-start(bf16[1024,100]{0,1:T(8,128)(2,1)} %param.19) | copy-start | bytes 614404
  7.2 5.1 %copy-start.5 = (f32[8,1024]{1,0:T(8,128)S(1)}, f32[8,1024]{1,0:T(8,128)}, u32[]{:S(2)}) copy-start(f32[8,1024]{1,0:T(8,128)} %mod.1) | copy-start | bytes 98308
  7.2 5.1 %copy-start.1 = (bf16[1024,1024]{1,0:T(8,128)(2,1)S(1)}, bf16[1024,1024]{1,0:T(8,128)(2,1)}, u32[]{:S(2)}) copy-start(bf16[1024,1024]{1,0:T(8,128)(2,1)} %w_up.1) | copy-start | bytes 6291460
  7.2 118.1 %all-gather.3.cloned.1.call-start = ((), (), s32[]{:S(2)}) async-start(), calls=%async_computation | async-start | bytes 4423680 | tf_op jit(solution)/shard_map/all_gather | solution.py:661
  7.9 117.3 %all-gather.5.cloned.1.call-start = ((), (), s32[]{:S(2)}) async-start(), calls=%async_computation.1 | async-start | bytes 4423680 | tf_op jit(solution)/shard_map/all_gather | solution.py:662
  12.3 1.4 copy-start.2
  13.7 1.0 copy-start.3
  14.8 1.0 copy-start.4
  124.3 1.0 copy-start
Sparse Core Ops, SparseCore 0:
  9.6 44.7 all-gather.2
  55.9 45.0 all-gather.4

commit v2 on v1

--- a/solution.py
+++ b/solution.py
@@ -136,6 +136,46 @@
         remote(own, own, self.d_send.at[i], self.d_recv.at[i], {"sub": self.here.sibling}).wait_recv()
 
 
+class WeightGather:
+    def __init__(self, here, own, whole, sems):
+        self.here, self.own, self.whole = here, own, whole
+        self.x_send, self.x_recv, self.d_send, self.d_recv = sems
+
+    def piece(self, block):
+        return self.whole.at[:, rows_of(block, self.own.shape[1])]
+
+    def local(self):
+        return pltpu.make_async_copy(self.own, self.piece(self.here.s), self.x_send.at[0])
+
+    def across(self, i):
+        here = self.here
+        ahead = lax.rem(here.chip + i, here.chips)
+        return remote(self.own, self.piece(here.s), self.x_send.at[i], self.x_recv.at[i], here.peer(ahead))
+
+    def forward(self, i):
+        piece = self.piece(self.here.block(i, False))
+        source = self.own if i == 0 else piece
+        return remote(source, piece, self.d_send.at[i], self.d_recv.at[i], {"sub": self.here.sibling})
+
+    def start(self):
+        for i in range(1, self.here.chips):
+            self.across(i).start()
+        self.forward(0).start()
+        self.local().start()
+
+    def pass_on(self):
+        for i in range(1, self.here.chips):
+            self.across(i).wait_recv()
+            self.forward(i).start()
+
+    def finish(self):
+        for i in range(self.here.chips):
+            self.forward(i).wait()
+        for i in range(1, self.here.chips):
+            self.across(i).wait_send()
+        self.local().wait()
+
+
 class Scatter:
     def __init__(self, here, buf, rows, near, far, sems):
         self.here, self.buf, self.rows, self.near, self.far = here, buf, rows, near, far
@@ -213,9 +253,9 @@
 
 
 def layer_kernel(
-    frames, mod, w_project, w_heads_out, w_up, w_down, w_velocity, noisy, mel_out,
+    frames, mod, w_project, w_heads_out, w_up, w_down, w_velocity, noisy, w_own, mel_out, w_all,
     h_one, h_two, queries, keys, values, attended, sums_one, sums_two, near_one, far_one, near_two,
-    far_two, mixed, mel_all, gather_sems, scatter_sems, look_send, look_recv,
+    far_two, mixed, mel_all, gather_sems, scatter_sems, weight_sems, look_send, look_recv,
 ):
     here = Place()
     rows, width = frames.shape
@@ -258,6 +298,9 @@
         lookback(keys, 0).start()
         lookback(values, 1).start()
 
+    weights = WeightGather(here, w_own, w_all, [weight_sems.at[j] for j in range(4)])
+    weights.start()
+
     @pl.when(first)
     def _():
         keys[pl.ds(0, BLK)] = jnp.zeros((BLK, keys.shape[1]), BF16)
@@ -266,9 +309,9 @@
     blocks = total_rows // BLK
     heads = queries.shape[1] // HEAD_DIM
 
-    def attend(turn, carry):
-        b = lax.rem(turn + 1, blocks)
-
+    scatter = Scatter(here, sums_one, rows, near_one, far_one, [scatter_sems.at[0, j] for j in range(4)])
+
+    def attend(b):
         @pl.when(jnp.logical_and(b == 0, jnp.logical_not(first)))
         def _():
             lookback(keys, 0).wait_recv()
@@ -285,15 +328,32 @@
             scale = 1.0 / jnp.sum(raised, axis=-1, keepdims=True)
             attended[:, cols] = (dot(raised.astype(BF16), values[both, cols]) * scale).astype(BF16)
         sums_one[at] = dot(attended[...], w_heads_out[...]).astype(BF16)
-        return carry
-
-    lax.fori_loop(0, blocks, attend, 0)
-
-    scatter = Scatter(here, sums_one, rows, near_one, far_one, [scatter_sems.at[0, j] for j in range(4)])
-    for i in reversed(range(here.chips)):
-        scatter.to_sibling(i).start()
-    for i in range(1, here.chips):
-        scatter.pass_on(i)
+
+    if rows == BLK:
+        def attend_step(p, carry):
+            i = here.chips - 1 - p
+            attend(here.block(i, True))
+            scatter.to_sibling(i).start()
+            attend(here.block(i, False))
+
+            @pl.when(i > 0)
+            def _():
+                scatter.pass_on(i)
+
+            return carry
+
+        lax.fori_loop(0, here.chips, attend_step, 0)
+    else:
+
+        def attend_turn(turn, carry):
+            attend(lax.rem(turn + 1, blocks))
+            return carry
+
+        lax.fori_loop(0, blocks, attend_turn, 0)
+        for i in reversed(range(here.chips)):
+            scatter.to_sibling(i).start()
+        for i in range(1, here.chips):
+            scatter.pass_on(i)
     scatter.arrive()
 
     def norm_two(q, carry):
@@ -306,6 +366,7 @@
     lax.fori_loop(0, steps, norm_two, 0)
     gather_two = Gather(here, h_two, rows, [gather_sems.at[1, j] for j in range(4)])
     gather_two.start()
+    weights.pass_on()
     scatter_two = Scatter(here, sums_two, rows, near_two, far_two, [scatter_sems.at[1, j] for j in range(4)])
 
     def feed_forward(block, i, other):
@@ -325,7 +386,7 @@
         final = (mixed[at_step(q)].astype(F32) + mod[5:6] * feed).astype(BF16)
         normed = norm_rows(final.astype(F32), mod[6:7], mod[7:8]).astype(BF16)
         own = at_step(q, here.s * rows)
-        mel_all[own] = noisy[own] + 0.5 * dot(normed, w_velocity[...])
+        mel_all[own] = noisy[own] + 0.5 * dot_t(normed, w_velocity[...])
         return carry
 
     lax.fori_loop(0, steps, step_mel, 0)
@@ -342,11 +403,11 @@
         lookback(keys, 0).wait_send()
         lookback(values, 1).wait_send()
 
-    for one in (gather, gather_two, gather_mel, scatter, scatter_two):
+    for one in (gather, gather_two, gather_mel, scatter, scatter_two, weights):
         one.finish()
 
 
-def layer(frames, modulation, w_project, w_heads_out, w_up, w_down, w_velocity, noisy_mel):
+def layer(frames, modulation, w_project, w_heads_out, w_up, w_down, w_velocity, noisy_mel, w_own):
     n = lax.axis_size("sub")
     rows, width = frames.shape
     total_rows = n * rows
@@ -355,9 +416,12 @@
     chips = n // 2
     return pl.pallas_call(
         layer_kernel,
-        out_shape=jax.ShapeDtypeStruct((total_rows, mel), F32),
-        in_specs=[pl.BlockSpec(memory_space=VMEM)] * 8,
-        out_specs=pl.BlockSpec(memory_space=VMEM),
+        out_shape=(
+            jax.ShapeDtypeStruct((total_rows, mel), F32),
+            jax.ShapeDtypeStruct((w_own.shape[0], n * w_own.shape[1], w_own.shape[2]), BF16),
+        ),
+        in_specs=[pl.BlockSpec(memory_space=VMEM)] * 8 + [pl.BlockSpec(memory_space=pl.ANY)],
+        out_specs=(pl.BlockSpec(memory_space=VMEM), pl.BlockSpec(memory_space=pl.ANY)),
         scratch_shapes=[
             VMEM((total_rows, width), BF16),
             VMEM((total_rows, width), BF16),
@@ -375,6 +439,7 @@
             VMEM((total_rows, mel), F32),
             DMA((3, 4, chips)),
             DMA((2, 4, chips)),
+            DMA((4, chips)),
             DMA((2,)),
             DMA((2,)),
         ],
@@ -383,13 +448,13 @@
         ),
         cost_estimate=pl.CostEstimate(flops=80 * 10**9, bytes_accessed=8 * 2**20, transcendentals=0),
         name="layer",
-    )(frames, modulation, w_project, w_heads_out, w_up, w_down, w_velocity, noisy_mel)
+    )(frames, modulation, w_project, w_heads_out, w_up, w_down, w_velocity, noisy_mel, w_own)
 
 
 def section_kernel(
-    mel, w_prelude, w_upsample, alpha, w_dilated, w_plain, out,
+    mel, w_prelude, w_upsample, alpha, w_dilated_all, w_plain_own, out,
     mel_wide, prelude, sums, near, far, up, taps, acts, woven, halo_low, halo_high,
-    scatter_sems, edge_send, edge_recv,
+    w_dilated, w_plain, scatter_sems, weight_sems, edge_send, edge_recv, load_sem,
 ):
     here = Place()
     total_rows, bands = mel.shape
@@ -407,6 +472,10 @@
     not_begin, not_end = spot > 0, spot < here.times * here.n - 1
     greet(here, ((not_first, behind), (not_last, ahead), (not_begin, earlier), (not_end, later)))
 
+    load = pltpu.make_async_copy(w_dilated_all, w_dilated, load_sem)
+    load.start()
+    weights = WeightGather(here, w_plain_own, w_plain, [weight_sems.at[j] for j in range(4)])
+
     zeros16 = jnp.zeros((16, bands), F32)
 
     mel_wide[pl.ds(0, 8)] = zeros16[:8]
@@ -438,9 +507,9 @@
 
     def prelude_rows(start, count):
         wide = mel_wide[pl.ds(start, count + 16)]
-        total = jnp.zeros((count, w_prelude.shape[1]), F32)
+        total = jnp.zeros((count, w_prelude.shape[2]), F32)
         for j in range(w_prelude.shape[0]):
-            total = total + dot_t(wide[5 + j : 5 + j + count].astype(BF16), w_prelude[j])
+            total = total + dot(wide[5 + j : 5 + j + count].astype(BF16), w_prelude[j])
         return total.astype(BF16).astype(F32)
 
     @pl.when(not_first)
@@ -508,6 +577,8 @@
     def _():
         down_send.start()
 
+    weights.start()
+
     @pl.when(begin)
     def _():
         halo_low[...] = jnp.zeros(halo_low.shape, BF16)
@@ -558,6 +629,8 @@
     line = lax.broadcasted_iota(jnp.int32, (length, 1), 0)
     outside = (begin & (line < 8)) | (end & (line >= rows + 8))
     row_mask = jnp.where(outside, 0.0, 1.0)
+
+    load.wait()
 
     def dilated_step(q, carry):
         cols = pl.ds(pl.multiple_of(q * chunk, chunk), chunk)
@@ -572,7 +645,9 @@
         return carry
 
     lax.fori_loop(0, mid // chunk, dilated_step, 0)
+    weights.pass_on()
     prepare((3,), (0,))
+    weights.finish()
 
     def plain_step(q, carry):
         cols = pl.ds(pl.multiple_of(q * chunk, chunk), chunk)
@@ -628,11 +703,11 @@
     return pl.pallas_call(
         section_kernel,
         out_shape=jax.ShapeDtypeStruct((4 * rows, mid), BF16),
-        in_specs=[pl.BlockSpec(memory_space=VMEM)] * 6,
+        in_specs=[pl.BlockSpec(memory_space=VMEM)] * 4 + [pl.BlockSpec(memory_space=pl.ANY)] * 2,
         out_specs=pl.BlockSpec(memory_space=VMEM),
         scratch_shapes=[
             VMEM((total_rows + 32, bands), F32),
-            VMEM((total_rows + 16, w_prelude.shape[1]), F32),
+            VMEM((total_rows + 16, w_prelude.shape[2]), F32),
             VMEM((total_rows, wide), BF16),
             VMEM((chips, rows, wide), BF16),
             VMEM((chips, rows, wide), BF16),
@@ -642,9 +717,13 @@
             VMEM((4, rows, mid), F32),
             VMEM((16, wide), BF16),
             VMEM((16, wide), BF16),
+            VMEM(w_dilated.shape, BF16),
+            VMEM(w_dilated.shape, BF16),
+            DMA((4, chips)),
             DMA((4, chips)),
             DMA((4,)),
             DMA((4,)),
+            DMA,
         ],
         compiler_params=pltpu.CompilerParams(
             collective_id=1, has_side_effects=True, vmem_limit_bytes=58 * 2**20
@@ -658,10 +737,12 @@
     frames, modulation, w_project, w_heads_out, w_up, w_down, w_velocity, noisy_mel, w_prelude,
     w_upsample, snake_alpha, w_dilated, w_plain,
 ):
-    dilated_all = lax.all_gather(w_dilated, "sub", axis=1, tiled=True)
-    plain_all = lax.all_gather(w_plain, "sub", axis=1, tiled=True)
-    mel_next = layer(frames, modulation, w_project, w_heads_out, w_up, w_down, w_velocity, noisy_mel)
-    section_out = section(mel_next, w_prelude, w_upsample, snake_alpha, dilated_all, plain_all)
+    mel_next, dilated_all = layer(
+        frames, modulation, w_project, w_heads_out, w_up, w_down, w_velocity.T, noisy_mel, w_dilated
+    )
+    section_out = section(
+        mel_next, jnp.swapaxes(w_prelude, 1, 2), w_upsample, snake_alpha, dilated_all, w_plain
+    )
     return (mel_next, section_out)
 
 

time: 211 us -> 189 us (0.90)
  between operations: 14.1 us -> 0.68 us
  Pallas kernels: 184 us -> 176 us
    pallas_call x1, Pallas kernels: 108 us -> 92 us  [layer(): pl.pallas_call(layer_kernel, out_shape=(jax.ShapeDtypeStruct((total_rows,...]
    pallas_call x1, Pallas kernels: 75.3 us -> 83.9 us  [section(): pl.pallas_call(section_kernel, out_shape=jax.ShapeDtypeStruct((4 * rows,...]
  transfers between devices with their start and end apart: 2 -> 0, of which waited for: 0 -> 0; matrix products, arithmetic and copies ran while one was open for 2% -> 0% of each run, Pallas kernels for 52% -> 0%
where the time goes in v2:
time: 189 us
  Pallas kernels  176 us (93%)
  local copies, waits for them, and re-layouts  12 us (6%)
    pallas_call x1, Pallas kernels, layer(): pl.pallas_call(layer_kernel, out_shape=(jax.ShapeDtypeStruct((total_rows,...  92 us
    pallas_call x1, Pallas kernels, section(): pl.pallas_call(section_kernel, out_shape=jax.ShapeDtypeStruct((4 * rows,...  83.9 us
    unnamed x19, local copies, waits for them, and re-layouts  12 us

profile of v2, /device:TPU:0, one launch (start us, length us, event | category | flops | bytes accessed | tf_op | source)
XLA Modules:
  0.0 188.6 jit_solution(8085506848646705821)
XLA Ops:
  0.6 1.2 copy.15.noisy
  1.8 0.0 copy-start.2
  1.9 1.4 copy-done.2
  3.3 0.0 copy-start.3
  3.3 1.2 copy-done.3
  4.4 0.0 copy-start.4
  4.4 1.0 copy-done.4
  5.5 0.0 copy-start.5
  5.5 1.0 copy-done.5
  6.5 0.0 copy-start.6
  6.5 0.9 copy-done.6
  7.4 0.0 copy-start.7
  7.4 0.8 copy-done.7
  8.2 92.0 %layer.1 = (f32[1024,100]{1,0:T(8,128)S(1)}, bf16[3,768,768]{2,1,0:T(8,128)(2,1)}) custom-call(bf16[256,1024]{1,0:T(8,128)(2,1)S(1)} %copy-done.4, f32[8,1024]{1,0:T(8,128)S(1)} %copy-done.7, bf16[3,1024,256]{2,1,0:T(8,128)(2,1)S(1)} %copy-done.2, bf16[256,1024]{1,0:T(8,128)(2,1)S(1)} %copy-done.5, bf16[1024,1024]{1,0:T(8,128)(2,1)} %w_up.1, ...), custom_call_target="tpu_custom_call" | custom-call | flops 80000000000 | bytes 8388608 | tf_op jit(solution)/shard_map/layer/pallas_call | solution.py:417
  100.2 0.0 copy-start
  100.2 0.8 copy-done
  101.0 0.0 copy-start.1
  101.0 83.9 %section.1 = bf16[1024,768]{1,0:T(8,128)(2,1)} custom-call(f32[1024,100]{1,0:T(8,128)} %copy-done, bf16[7,100,384]{2,1,0:T(8,128)(2,1)} %bitcast.3, bf16[8,384,768]{2,1,0:T(8,128)(2,1)} %w_upsample.1, f32[2,768]{1,0:T(2,128)} %alpha.1, bf16[3,768,768]{2,1,0:T(8,128)(2,1)} %get-tuple-element.5.w_dilated_all, bf16[3,192,768]{2,1,0:T(8,128)(2,1)} %w_plain_own.1), custom_call_target="tpu_custom_call" | custom-call | flops 60000002048 | bytes 16777216 | tf_op jit(solution)/shard_map/section/pallas_call | solution.py:703
  185.0 0.0 copy-done.1
  185.0 1.0 copy.16
  186.0 2.7 %copy.18 = bf16[1024,768]{1,0:T(8,128)(2,1)} copy(bf16[1024,768]{1,0:T(8,128)(2,1)} %section.1) | data formatting | bytes 3145728
Async XLA Ops:
  1.8 1.4 copy-start.2
  3.3 1.2 copy-start.3
  4.4 1.0 copy-start.4
  5.5 1.0 copy-start.5
  6.5 0.9 copy-start.6
  7.4 0.8 copy-start.7
  100.2 0.8 copy-start
  101.0 84.0 %copy-start.1 = (f32[1024,100]{1,0:T(8,128)S(1)}, f32[1024,100]{1,0:T(8,128)}, u32[]{:S(2)}) copy-start(f32[1024,100]{1,0:T(8,128)} %copy-done) | copy-start | bytes 1228804

commit v3 on v2

--- a/solution.py
+++ b/solution.py
@@ -139,10 +139,17 @@
 class WeightGather:
     def __init__(self, here, own, whole, sems):
         self.here, self.own, self.whole = here, own, whole
-        self.x_send, self.x_recv, self.d_send, self.d_recv = sems
+        self.x_send, self.x_recv, self.d_send, self.d_recv, self.t_send, self.t_recv = sems
+        half = own.shape[2] // 2
+        odd = lax.rem(here.t, 2)
+        self.cols = pl.ds(pl.multiple_of(odd * half, half), half)
+        self.partner = {"tm": here.t + 1 - 2 * odd}
+
+    def rows(self, block):
+        return rows_of(block, self.own.shape[1])
 
     def piece(self, block):
-        return self.whole.at[:, rows_of(block, self.own.shape[1])]
+        return self.whole.at[:, self.rows(block)]
 
     def local(self):
         return pltpu.make_async_copy(self.own, self.piece(self.here.s), self.x_send.at[0])
@@ -150,7 +157,13 @@
     def across(self, i):
         here = self.here
         ahead = lax.rem(here.chip + i, here.chips)
-        return remote(self.own, self.piece(here.s), self.x_send.at[i], self.x_recv.at[i], here.peer(ahead))
+        source = self.own.at[:, :, self.cols]
+        target = self.whole.at[:, self.rows(here.s), self.cols]
+        return remote(source, target, self.x_send.at[i], self.x_recv.at[i], here.peer(ahead))
+
+    def along(self, i):
+        half = self.whole.at[:, self.rows(self.here.block(i, False)), self.cols]
+        return remote(half, half, self.t_send.at[i], self.t_recv.at[i], self.partner)
 
     def forward(self, i):
         piece = self.piece(self.here.block(i, False))
@@ -163,9 +176,14 @@
         self.forward(0).start()
         self.local().start()
 
+    def exchange(self):
+        for i in range(1, self.here.chips):
+            self.across(i).wait_recv()
+            self.along(i).start()
+
     def pass_on(self):
         for i in range(1, self.here.chips):
-            self.across(i).wait_recv()
+            self.along(i).wait_recv()
             self.forward(i).start()
 
     def finish(self):
@@ -173,6 +191,7 @@
             self.forward(i).wait()
         for i in range(1, self.here.chips):
             self.across(i).wait_send()
+            self.along(i).wait_send()
         self.local().wait()
 
 
@@ -253,9 +272,10 @@
 
 
 def layer_kernel(
-    frames, mod, w_project, w_heads_out, w_up, w_down, w_velocity, noisy, w_own, mel_out, w_all,
+    frames, mod, project_in, heads_out_in, up_in, down_in, w_velocity, noisy, w_own, mel_out, w_all,
     h_one, h_two, queries, keys, values, attended, sums_one, sums_two, near_one, far_one, near_two,
-    far_two, mixed, mel_all, gather_sems, scatter_sems, weight_sems, look_send, look_recv,
+    far_two, mixed, mel_all, gather_sems, scatter_sems, weight_sems, load_sems, w_project, w_heads_out, w_up, w_down,
+    look_send, look_recv,
 ):
     here = Place()
     rows, width = frames.shape
@@ -264,6 +284,10 @@
     steps = rows // step
     first, last = here.t == 0, here.t == here.times - 1
     behind, ahead = {"tm": here.t - 1}, {"tm": here.t + 1}
+    held = ((project_in, w_project), (heads_out_in, w_heads_out), (up_in, w_up), (down_in, w_down))
+    loads = [pltpu.make_async_copy(*pair, load_sems.at[j]) for j, pair in enumerate(held)]
+    for load in loads:
+        load.start()
     greet(here, ((here.t > 0, behind), (here.t < here.times - 1, ahead)))
 
     def at_step(q, base=0):
@@ -286,6 +310,7 @@
         keys[later] = dot(h, w_project[1]).astype(BF16)
         values[later] = dot(h, w_project[2]).astype(BF16)
 
+    loads[0].wait()
     gather.each(project)
 
     def lookback(buf, j):
@@ -298,7 +323,7 @@
         lookback(keys, 0).start()
         lookback(values, 1).start()
 
-    weights = WeightGather(here, w_own, w_all, [weight_sems.at[j] for j in range(4)])
+    weights = WeightGather(here, w_own, w_all, [weight_sems.at[j] for j in range(6)])
     weights.start()
 
     @pl.when(first)
@@ -310,6 +335,8 @@
     heads = queries.shape[1] // HEAD_DIM
 
     scatter = Scatter(here, sums_one, rows, near_one, far_one, [scatter_sems.at[0, j] for j in range(4)])
+
+    loads[1].wait()
 
     def attend(b):
         @pl.when(jnp.logical_and(b == 0, jnp.logical_not(first)))
@@ -354,6 +381,7 @@
             scatter.to_sibling(i).start()
         for i in range(1, here.chips):
             scatter.pass_on(i)
+    weights.exchange()
     scatter.arrive()
 
     def norm_two(q, carry):
@@ -376,6 +404,8 @@
         if other:
             scatter_two.to_sibling(i).start()
 
+    loads[2].wait()
+    loads[3].wait()
     gather_two.each(feed_forward)
     for i in range(1, here.chips):
         scatter_two.pass_on(i)
@@ -420,7 +450,10 @@
             jax.ShapeDtypeStruct((total_rows, mel), F32),
             jax.ShapeDtypeStruct((w_own.shape[0], n * w_own.shape[1], w_own.shape[2]), BF16),
         ),
-        in_specs=[pl.BlockSpec(memory_space=VMEM)] * 8 + [pl.BlockSpec(memory_space=pl.ANY)],
+        in_specs=[
+            pl.BlockSpec(memory_space=space)
+            for space in [VMEM] * 2 + [pl.ANY] * 4 + [VMEM] * 2 + [pl.ANY]
+        ],
         out_specs=(pl.BlockSpec(memory_space=VMEM), pl.BlockSpec(memory_space=pl.ANY)),
         scratch_shapes=[
             VMEM((total_rows, width), BF16),
@@ -439,12 +472,17 @@
             VMEM((total_rows, mel), F32),
             DMA((3, 4, chips)),
             DMA((2, 4, chips)),
-            DMA((4, chips)),
+            DMA((6, chips)),
+            DMA((4,)),
+            VMEM(w_project.shape, BF16),
+            VMEM(w_heads_out.shape, BF16),
+            VMEM(w_up.shape, BF16),
+            VMEM(w_down.shape, BF16),
             DMA((2,)),
             DMA((2,)),
         ],
         compiler_params=pltpu.CompilerParams(
-            collective_id=0, has_side_effects=True, vmem_limit_bytes=48 * 2**20
+            collective_id=0, has_side_effects=True, vmem_limit_bytes=60 * 2**20
         ),
         cost_estimate=pl.CostEstimate(flops=80 * 10**9, bytes_accessed=8 * 2**20, transcendentals=0),
         name="layer",
@@ -452,9 +490,9 @@
 
 
 def section_kernel(
-    mel, w_prelude, w_upsample, alpha, w_dilated_all, w_plain_own, out,
+    mel, w_prelude, w_upsample_in, alpha, w_dilated_all, w_plain_own, out,
     mel_wide, prelude, sums, near, far, up, taps, acts, woven, halo_low, halo_high,
-    w_dilated, w_plain, scatter_sems, weight_sems, edge_send, edge_recv, load_sem,
+    w_dilated, w_plain, w_upsample, scatter_sems, weight_sems, edge_send, edge_recv, load_sems,
 ):
     here = Place()
     total_rows, bands = mel.shape
@@ -470,11 +508,13 @@
     earlier = {"tm": low_spot // here.n, "sub": lax.rem(low_spot, here.n)}
     later = {"tm": high_spot // here.n, "sub": lax.rem(high_spot, here.n)}
     not_begin, not_end = spot > 0, spot < here.times * here.n - 1
+    load_up = pltpu.make_async_copy(w_upsample_in, w_upsample, load_sems.at[0])
+    load_up.start()
+    load = pltpu.make_async_copy(w_dilated_all, w_dilated, load_sems.at[1])
+    load.start()
     greet(here, ((not_first, behind), (not_last, ahead), (not_begin, earlier), (not_end, later)))
 
-    load = pltpu.make_async_copy(w_dilated_all, w_dilated, load_sem)
-    load.start()
-    weights = WeightGather(here, w_plain_own, w_plain, [weight_sems.at[j] for j in range(4)])
+    weights = WeightGather(here, w_plain_own, w_plain, [weight_sems.at[j] for j in range(6)])
 
     zeros16 = jnp.zeros((16, bands), F32)
 
@@ -504,6 +544,8 @@
     @pl.when(not_first)
     def _():
         mel_down.start()
+
+    weights.start()
 
     def prelude_rows(start, count):
         wide = mel_wide[pl.ds(start, count + 16)]
@@ -554,7 +596,9 @@
 
         return carry
 
+    load_up.wait()
     lax.fori_loop(0, here.chips, upsample_step, 0)
+    weights.exchange()
     scatter.arrive()
 
     step = min(64, rows)
@@ -577,7 +621,7 @@
     def _():
         down_send.start()
 
-    weights.start()
+    weights.pass_on()
 
     @pl.when(begin)
     def _():
@@ -645,7 +689,6 @@
         return carry
 
     lax.fori_loop(0, mid // chunk, dilated_step, 0)
-    weights.pass_on()
     prepare((3,), (0,))
     weights.finish()
 
@@ -703,7 +746,9 @@
     return pl.pallas_call(
         section_kernel,
         out_shape=jax.ShapeDtypeStruct((4 * rows, mid), BF16),
-        in_specs=[pl.BlockSpec(memory_space=VMEM)] * 4 + [pl.BlockSpec(memory_space=pl.ANY)] * 2,
+        in_specs=[
+            pl.BlockSpec(memory_space=space) for space in [VMEM] * 2 + [pl.ANY, VMEM] + [pl.ANY] * 2
+        ],
         out_specs=pl.BlockSpec(memory_space=VMEM),
         scratch_shapes=[
             VMEM((total_rows + 32, bands), F32),
@@ -719,11 +764,12 @@
             VMEM((16, wide), BF16),
             VMEM(w_dilated.shape, BF16),
             VMEM(w_dilated.shape, BF16),
+            VMEM(w_upsample.shape, BF16),
             DMA((4, chips)),
-            DMA((4, chips)),
+            DMA((6, chips)),
             DMA((4,)),
             DMA((4,)),
-            DMA,
+            DMA((2,)),
         ],
         compiler_params=pltpu.CompilerParams(
             collective_id=1, has_side_effects=True, vmem_limit_bytes=58 * 2**20

time: 189 us -> 159 us (0.84)
  Pallas kernels: 176 us -> 152 us
  local copies, waits for them, and re-layouts: 12 us -> 5.64 us
    pallas_call x1, Pallas kernels: 83.9 us -> 69.2 us  [section(): pl.pallas_call(section_kernel, out_shape=jax.ShapeDtypeStruct((4 * rows,...]
    pallas_call x1, Pallas kernels: 92 us -> 83.1 us  [layer(): pl.pallas_call(layer_kernel, out_shape=(jax.ShapeDtypeStruct((total_rows,...]
    unnamed x19 -> x5, local copies, waits for them, and re-layouts: 12 us -> 5.64 us
where the time goes in v3:
time: 159 us
  Pallas kernels  152 us (96%)
  local copies, waits for them, and re-layouts  5.64 us (4%)
    pallas_call x1, Pallas kernels, layer(): pl.pallas_call(layer_kernel, out_shape=(jax.ShapeDtypeStruct((total_rows,...  83.1 us
    pallas_call x1, Pallas kernels, section(): pl.pallas_call(section_kernel, out_shape=jax.ShapeDtypeStruct((4 * rows,...  69.2 us
    unnamed x5, local copies, waits for them, and re-layouts  5.64 us

profile of v3, /device:TPU:0, one launch (start us, length us, event | category | flops | bytes accessed | tf_op | source)
XLA Modules:
  0.0 158.6 jit_solution(5460071582604251929)
XLA Ops:
  0.6 2.0 %copy.15.noisy = f32[1024,100]{1,0:T(8,128)} copy(f32[1024,100]{0,1:T(8,128)} %param.20) | data formatting | bytes 819200 | tf_op args[7]
  2.6 83.1 %layer.1 = (f32[1024,100]{1,0:T(8,128)}, bf16[3,768,768]{2,1,0:T(8,128)(2,1)}) custom-call(bf16[256,1024]{1,0:T(8,128)(2,1)} %frames.1, f32[8,1024]{1,0:T(8,128)} %mod.1, bf16[3,1024,256]{2,1,0:T(8,128)(2,1)} %project_in.1, bf16[256,1024]{1,0:T(8,128)(2,1)} %heads_out_in.1, bf16[1024,1024]{1,0:T(8,128)(2,1)} %up_in.1, bf16[1024,1024]{1,0:T(8,128)(2,1)} %down_in.1, ...), custom_call_target="tpu_custom_call" | custom-call | flops 80000000000 | bytes 8388608 | tf_op jit(solution)/shard_map/layer/pallas_call | solution.py:447
  85.7 0.0 copy-start
  85.7 69.2 %section.1 = bf16[1024,768]{1,0:T(8,128)(2,1)} custom-call(f32[1024,100]{1,0:T(8,128)} %get-tuple-element.6.mel, bf16[7,100,384]{2,1,0:T(8,128)(2,1)} %bitcast.2, bf16[8,384,768]{2,1,0:T(8,128)(2,1)} %w_upsample_in.1, f32[2,768]{1,0:T(2,128)} %alpha.1, bf16[3,768,768]{2,1,0:T(8,128)(2,1)} %get-tuple-element.5.w_dilated_all, bf16[3,192,768]{2,1,0:T(8,128)(2,1)} %w_plain_own.1), custom_call_target="tpu_custom_call" | custom-call | flops 60000002048 | bytes 16777216 | tf_op jit(solution)/shard_map/section/pallas_call | solution.py:746
  155.0 0.0 copy-done
  155.0 1.0 copy.16
  156.0 2.7 %copy.18 = bf16[1024,768]{1,0:T(8,128)(2,1)} copy(bf16[1024,768]{1,0:T(8,128)(2,1)} %section.1) | data formatting | bytes 3145728
Async XLA Ops:
  85.7 69.2 %copy-start = (f32[1024,100]{1,0:T(8,128)S(1)}, f32[1024,100]{1,0:T(8,128)}, u32[]{:S(2)}) copy-start(f32[1024,100]{1,0:T(8,128)} %get-tuple-element.6.mel) | copy-start | bytes 1228804
